TPU v7x, 32 devices: a whole 2x2x4 slice. The times are simulated.
32 devices in a mesh: cfg: 2 (over core), seq: 4 (over z), blk: 4 (over y, x).
Axes of the slice: x: 2, y: 2, z: 4, core: 2. Of those that a mesh axis runs over, the one named last changes fastest.
Arguments:
- img_hidden: bfloat16 [2, 2, 2048, 1536], P('cfg', None, 'seq', 'blk'), may hold values from -15 to 15
- txt_hidden: bfloat16 [2, 2, 160, 1536], P('cfg', None, 'seq', 'blk'), may hold values from -6 to 6
- img_mod: float32 [2, 2, 6, 1536], P('cfg'), may hold values from -9 to 9
- txt_mod: float32 [2, 2, 2, 1536], P('cfg'), may hold values from -3 to 3
- out_mod: float32 [2, 2, 2, 1536], P('cfg'), may hold values from -3 to 3
- w_qkv: bfloat16 [3, 1536, 1536], P(None, None, 'blk'), may hold values from -0.25 to 0.25
- w_txt_kv: bfloat16 [2, 1536, 1536], P(None, None, 'blk'), may hold values from -0.25 to 0.25
- w_out: bfloat16 [1536, 1536], P('blk'), may hold values from -0.15625 to 0.15625
- w_fc1: bfloat16 [1536, 6144], P(None, 'blk'), may hold values from -0.15625 to 0.15625
- w_fc2: bfloat16 [6144, 1536], P('blk'), may hold values from -0.078125 to 0.078125
- w_proj: bfloat16 [1536, 64], P('blk'), may hold values from -0.15625 to 0.15625
- latent: float32 [2, 2048, 64], P(None, 'seq', 'cfg'), may hold values from -6 to 6
- lengths: int32 [2, 2], P('cfg'), may hold values from 1 to 154, as said below
- t_index: int32 [2], replicated, may hold values from 0 to 24
- stride: int32 [2], replicated, may hold values from 1 to 4
- guide: float32 [2], replicated, may hold values from 4 to 8
Outputs:
- new_latent: float32 [2, 2048, 64], P(None, 'seq', 'cfg')
- update_max: float32 [2], replicated
Inputs may be any that keep to these rules, and one draw needn't show every extreme that they name: `lengths`: at least one entry equals 154.
All inputs are finite; a program needn't handle non-finite values.
Results may differ from a plain program's by a relative error of at most 0.015.
Values may be sent and summed in bfloat16 or wider, within the bound.
A program may use at most 192 MiB of HBM per device.

v0:
```python
import jax
import jax.numpy as jnp
from jax import lax
from jax.sharding import PartitionSpec as P

HEAD = 64
STEPS = 28
EPSILON = 1e-06
BLOCK_ROWS = 512


def from_partner(value, axis, bit):
    return lax.ppermute(value, axis, [(i, i ^ 1 << bit) for i in range(lax.axis_size(axis))])


def normalize(values):
    values = values.astype(jnp.float32)
    center = jnp.mean(values, axis=-1, keepdims=True)
    spread = jnp.mean(jnp.square(values - center), axis=-1, keepdims=True)
    return (values - center) * lax.rsqrt(spread + EPSILON)


def modulate(values, scale_row, shift_row):
    return (normalize(values) * (1.0 + scale_row[:, None, :]) + shift_row[:, None, :]).astype(
        jnp.bfloat16
    )


def project(values, weight):
    flat_rows = values.reshape(-1, values.shape[-1])
    result = jnp.dot(flat_rows, weight, preferred_element_type=jnp.float32)
    return result.reshape(values.shape[:-1] + (weight.shape[-1],))


def noise_level(step_index):
    remain = 1.0 - step_index.astype(jnp.float32) / STEPS
    return 3.0 * remain / (1.0 + 2.0 * remain)


def own_columns(values, column_block, shard_width):
    return lax.dynamic_slice_in_dim(
        values, column_block * shard_width, shard_width, values.ndim - 1
    )


def per_device(
    img_hidden,
    txt_hidden,
    img_mod,
    txt_mod,
    out_mod,
    w_qkv,
    w_txt_kv,
    w_out,
    w_fc1,
    w_fc2,
    w_proj,
    latent,
    lengths,
    t_index,
    stride,
    guide,
):
    column_block = lax.axis_index("blk")
    shard_width = img_hidden.shape[3]
    model_width = shard_width * lax.axis_size("blk")
    image_full, text_full = (
        lax.all_gather(img_hidden[0], "blk", axis=2, tiled=True),
        lax.all_gather(txt_hidden[0], "blk", axis=2, tiled=True),
    )
    image_mod = img_mod[0]
    prompts = image_full.shape[0]
    img_rows = image_full.shape[1]
    attn_in = modulate(image_full, image_mod[:, 1], image_mod[:, 0])
    queries = project(attn_in, w_qkv[0]).astype(jnp.bfloat16)
    keys_img = project(attn_in, w_qkv[1]).astype(jnp.bfloat16)
    values_img = project(attn_in, w_qkv[2]).astype(jnp.bfloat16)
    text_norm = modulate(text_full, txt_mod[0][:, 0], txt_mod[0][:, 1])
    text_keys = project(text_norm, w_txt_kv[0]).astype(jnp.bfloat16)
    text_values = project(text_norm, w_txt_kv[1]).astype(jnp.bfloat16)
    head_width = queries.shape[2]
    head_count = head_width // HEAD
    query_heads = queries.reshape(prompts, img_rows, head_count, HEAD)
    text_limit = lengths[0]

    def attend_block(running_state, key_block, value_block, live_mask):
        accumulated, running, denominator = running_state
        key_count = key_block.shape[1]
        key_heads = key_block.reshape(prompts, key_count, head_count, HEAD)
        value_heads = value_block.reshape(prompts, key_count, head_count, HEAD)
        scores = jnp.einsum(
            "pqhe,pkhe->phqk", query_heads, key_heads, preferred_element_type=jnp.float32
        ) * HEAD ** (-0.5)
        if live_mask is not None:
            scores = jnp.where(live_mask[:, None, None, :], scores, -jnp.inf)
        updated = jnp.maximum(running, jnp.max(scores, axis=-1))
        factor = jnp.exp(running - updated)
        weights = jnp.exp(scores - updated[..., None])
        denominator = denominator * factor + jnp.sum(weights, axis=-1)
        mixed_values = jnp.einsum(
            "phqk,pkhe->phqe",
            weights.astype(jnp.bfloat16),
            value_heads,
            preferred_element_type=jnp.float32,
        )
        accumulated = accumulated * factor[..., None] + mixed_values
        return (accumulated, updated, denominator)

    initial = (
        jnp.zeros((prompts, head_count, img_rows, HEAD), jnp.float32),
        jnp.full((prompts, head_count, img_rows), -1e30, jnp.float32),
        jnp.zeros((prompts, head_count, img_rows), jnp.float32),
    )
    running_state = initial
    key_piece = lax.all_gather(keys_img, "seq", axis=1, tiled=True)
    value_piece = lax.all_gather(values_img, "seq", axis=1, tiled=True)
    key_count = key_piece.shape[1]
    blocks = key_count // BLOCK_ROWS
    key_split = key_piece.reshape(prompts, blocks, BLOCK_ROWS, head_width).transpose(1, 0, 2, 3)
    value_split = value_piece.reshape(prompts, blocks, BLOCK_ROWS, head_width).transpose(1, 0, 2, 3)

    def scan_step(state_now, operands):
        key_block, value_block = operands
        return (attend_block(state_now, key_block, value_block, None), None)

    running_state, unused = lax.scan(scan_step, running_state, (key_split, value_split))
    all_text_keys, all_text_values = (
        lax.all_gather(text_keys, "seq", axis=1, tiled=True),
        lax.all_gather(text_values, "seq", axis=1, tiled=True),
    )
    slot_index = jnp.arange(all_text_keys.shape[1], dtype=jnp.int32)
    text_mask = slot_index[None, :] < text_limit[:, None]
    accumulated, running, denominator = attend_block(
        running_state, all_text_keys, all_text_values, text_mask
    )
    attended = (accumulated / denominator[..., None]).astype(jnp.bfloat16)
    attended = attended.transpose(0, 2, 1, 3).reshape(prompts, img_rows, head_width)
    attn_part = project(attended, w_out)
    attn_sum = lax.psum(attn_part.astype(jnp.bfloat16), "blk").astype(jnp.float32)
    resid_full = (image_full.astype(jnp.float32) + image_mod[:, 2][:, None, :] * attn_sum).astype(
        jnp.bfloat16
    )
    resid_one = own_columns(resid_full, column_block, shard_width)
    mlp_in = modulate(resid_full, image_mod[:, 4], image_mod[:, 3])
    hidden_units = jax.nn.gelu(project(mlp_in, w_fc1), approximate=True).astype(jnp.bfloat16)
    mlp_sum = lax.psum_scatter(
        project(hidden_units, w_fc2).astype(jnp.bfloat16), "blk", scatter_dimension=2, tiled=True
    ).astype(jnp.float32)
    gate_mlp = own_columns(image_mod[:, 5], column_block, shard_width)
    resid_two = (resid_one.astype(jnp.float32) + gate_mlp[:, None, :] * mlp_sum).astype(
        jnp.bfloat16
    )
    stream = resid_two.astype(jnp.float32)
    row_sum, row_squares = lax.psum(
        (jnp.sum(stream, axis=-1), jnp.sum(stream * stream, axis=-1)), "blk"
    )
    center = row_sum / model_width
    spread = row_squares / model_width - center * center
    final_mod = out_mod[0]
    final_scale = own_columns(final_mod[:, 0], column_block, shard_width)
    final_shift = own_columns(final_mod[:, 1], column_block, shard_width)
    final_in = (
        (stream - center[..., None])
        * lax.rsqrt(spread[..., None] + EPSILON)
        * (1.0 + final_scale[:, None, :])
        + final_shift[:, None, :]
    ).astype(jnp.bfloat16)
    velocity_part = project(final_in, w_proj)
    half_index = lax.axis_index("cfg")
    channel_width = latent.shape[2]
    guide_scale = guide[:, None, None]
    velocity = lax.psum(velocity_part.astype(jnp.bfloat16), "blk").astype(jnp.float32)
    outgoing = own_columns(velocity, 1 - half_index, channel_width)
    other_half = from_partner(outgoing.astype(jnp.bfloat16), "cfg", 0).astype(outgoing.dtype)
    own_half = own_columns(velocity, half_index, channel_width)
    velocity_cond = jnp.where(half_index == 0, own_half, other_half)
    velocity_uncond = jnp.where(half_index == 0, other_half, own_half)
    guided = velocity_uncond + guide_scale * (velocity_cond - velocity_uncond)
    step_size = noise_level(t_index + stride) - noise_level(t_index)
    update = step_size[:, None, None] * guided
    new_latent = latent + update
    local_peak = jnp.max(jnp.abs(update), axis=(1, 2))
    peak_value = lax.pmax(local_peak, ("cfg", "seq"))
    return (new_latent, peak_value)


def solution(mesh):
    placed = (
        P("cfg", None, "seq", "blk"),
        P("cfg", None, "seq", "blk"),
        P("cfg", None, None, None),
        P("cfg", None, None, None),
        P("cfg", None, None, None),
        P(None, None, "blk"),
        P(None, None, "blk"),
        P("blk", None),
        P(None, "blk"),
        P("blk", None),
        P("blk", None),
        P(None, "seq", "cfg"),
        P("cfg", None),
        P(),
        P(),
        P(),
    )
    return jax.shard_map(
        per_device,
        mesh=mesh,
        in_specs=placed,
        out_specs=(P(None, "seq", "cfg"), P()),
        check_vma=False,
    )
```

profile of v0, /device:TPU:0, one launch (start us, length us, event | category | flops | bytes accessed | tf_op | source)
XLA Modules:
  0.0 552.0 jit_solution(2850391820597721948)
XLA Ops:
  9.6 46.8 %all-gather.10.cloned.1.call-done = bf16[1,2,512,1536]{3,2,1,0:T(8,128)(2,1)} async-done(((bf16[1,2,512,384]{3,2,1,0:T(8,128)(2,1)}), bf16[1,2,512,1536]{3,2,1,0:T(8,128)(2,1)}) %all-gather.10.cloned.1.call-update) | async-done | bytes 3145744 | tf_op jit(solution)/shard_map/all_gather | solution.py:68
  64.4 5.0 convolution_convert_fusion.3
  69.5 9.2 %all-gather.1 = bf16[1,2,40,1536]{3,2,1,0:T(8,128)(2,1)S(1)} all-gather(bf16[1,2,40,384]{3,2,1,0:T(8,128)(2,1)S(1)} %copy-done.12), channel_id=3, replica_groups=mesh['cfg'=2,'seq'=4,'blk'=4] {'blk'}, dimensions={3}, use_global_device_ids=true | all-gather | bytes 307200 | tf_op jit(solution)/shard_map/all_gather | solution.py:69
  80.8 16.4 %all_gather.22 = bf16[2,160,384]{2,1,0:T(8,128)(2,1)} all-gather(bf16[2,40,384]{2,1,0:T(8,128)(2,1)S(1)} %fusion.79), channel_id=1, replica_groups=mesh['cfg'=2,'seq'=4,'blk'=4] {'seq'}, dimensions={1}, use_global_device_ids=true | all-gather | bytes 307200 | tf_op jit(solution)/shard_map/all_gather | solution.py:128
  100.0 16.7 %all_gather.23 = bf16[2,160,384]{2,1,0:T(8,128)(2,1)S(1)} all-gather(bf16[2,40,384]{2,1,0:T(8,128)(2,1)S(1)} %fusion.82), channel_id=1, replica_groups=mesh['cfg'=2,'seq'=4,'blk'=4] {'seq'}, dimensions={1}, use_global_device_ids=true | all-gather | bytes 307200 | tf_op jit(solution)/shard_map/all_gather | solution.py:129
  125.9 9.6 %all-gather.8.cloned.1.call-done = bf16[2,2048,384]{2,1,0:T(8,128)(2,1)} async-done(((bf16[2,512,384]{2,1,0:T(8,128)(2,1)}), bf16[2,2048,384]{2,1,0:T(8,128)(2,1)}) %all-gather.8.cloned.1.call-update) | async-done | bytes 3145744 | tf_op jit(solution)/shard_map/all_gather | solution.py:116
  140.2 59.2 %all-gather.6.cloned.1.call-done = bf16[2,2048,384]{2,1,0:T(8,128)(2,1)} async-done(((bf16[2,512,384]{2,1,0:T(8,128)(2,1)}), bf16[2,2048,384]{2,1,0:T(8,128)(2,1)}) %all-gather.6.cloned.1.call-update) | async-done | bytes 3145744 | tf_op jit(solution)/shard_map/all_gather | solution.py:115
  199.4 4.7 copy.36
  204.1 87.5 %while.15 = (s32[]{:T(128)}, f32[2,6,512,64]{2,3,1,0:T(8,128)S(1)}, f32[2,6,512]{2,1,0:T(8,128)}, f32[2,6,512]{2,1,0:T(8,128)}, bf16[4,2,512,384]{2,3,1,0:T(8,12...) while((s32[]{:T(128)}, f32[2,6,512,64]{2,3,1,0:T(8,128)S(1)}, ...), condition=%wide.region_5.0_spmd.clone, body=%wide.region_2.5_spmd.clone.sunk | while | flops 831682560 | bytes 97419496 | solution.py:126
  205.5 8.1 %bitcast_reduce_fusion.2 = (f32[2,6,512]{2,1,0:T(8,128)}, f32[2,6,512,512]{3,2,1,0:T(8,128)}) fusion(bf16[2,512,6,64]{1,3,2,0:T(8,128)(2,1)S(1)} %bitcast.165, bf16[2,512,6,64]{1,3,2,0:T(8,128)(2,1)} %get-tuple-element.199), kind=kOutput, calls=%fused_computation.1.clone.1 | convolution fusion | flops 408938496 | bytes 14180352 | tf_op jit(solution)/shard_map/while/body/eval_jaxpr/pqhe,pkhe->phqk/dot_general | solution.py:91
  214.4 6.8 %fusion.134 = f32[2,6,512]{2,1,0:T(8,128)S(1)} fusion(f32[2,6,512,512]{3,2,1,0:T(8,128)} %get-tuple-element.172, f32[2,6,512]{2,1,0:T(8,128)S(1)} %select_maximum_fusion.2), kind=kLoop, calls=%fused_computation.3.clone.1 | loop fusion | flops 9431040 | bytes 12632064 | tf_op jit(solution)/shard_map/while/body/eval_jaxpr/reduce_sum | solution.py:99
  227.4 8.1 %bitcast_reduce_fusion.2 = (f32[2,6,512]{2,1,0:T(8,128)}, f32[2,6,512,512]{3,2,1,0:T(8,128)}) fusion(bf16[2,512,6,64]{1,3,2,0:T(8,128)(2,1)S(1)} %bitcast.165, bf16[2,512,6,64]{1,3,2,0:T(8,128)(2,1)} %get-tuple-element.199), kind=kOutput, calls=%fused_computation.1.clone.1 | convolution fusion | flops 408938496 | bytes 14180352 | tf_op jit(solution)/shard_map/while/body/eval_jaxpr/pqhe,pkhe->phqk/dot_general | solution.py:91
  236.3 6.8 %fusion.134 = f32[2,6,512]{2,1,0:T(8,128)S(1)} fusion(f32[2,6,512,512]{3,2,1,0:T(8,128)} %get-tuple-element.172, f32[2,6,512]{2,1,0:T(8,128)S(1)} %select_maximum_fusion.2), kind=kLoop, calls=%fused_computation.3.clone.1 | loop fusion | flops 9431040 | bytes 12632064 | tf_op jit(solution)/shard_map/while/body/eval_jaxpr/reduce_sum | solution.py:99
  249.3 8.1 %bitcast_reduce_fusion.2 = (f32[2,6,512]{2,1,0:T(8,128)}, f32[2,6,512,512]{3,2,1,0:T(8,128)}) fusion(bf16[2,512,6,64]{1,3,2,0:T(8,128)(2,1)S(1)} %bitcast.165, bf16[2,512,6,64]{1,3,2,0:T(8,128)(2,1)} %get-tuple-element.199), kind=kOutput, calls=%fused_computation.1.clone.1 | convolution fusion | flops 408938496 | bytes 14180352 | tf_op jit(solution)/shard_map/while/body/eval_jaxpr/pqhe,pkhe->phqk/dot_general | solution.py:91
  258.2 6.8 %fusion.134 = f32[2,6,512]{2,1,0:T(8,128)S(1)} fusion(f32[2,6,512,512]{3,2,1,0:T(8,128)} %get-tuple-element.172, f32[2,6,512]{2,1,0:T(8,128)S(1)} %select_maximum_fusion.2), kind=kLoop, calls=%fused_computation.3.clone.1 | loop fusion | flops 9431040 | bytes 12632064 | tf_op jit(solution)/shard_map/while/body/eval_jaxpr/reduce_sum | solution.py:99
  271.2 8.1 %bitcast_reduce_fusion.2 = (f32[2,6,512]{2,1,0:T(8,128)}, f32[2,6,512,512]{3,2,1,0:T(8,128)}) fusion(bf16[2,512,6,64]{1,3,2,0:T(8,128)(2,1)S(1)} %bitcast.165, bf16[2,512,6,64]{1,3,2,0:T(8,128)(2,1)} %get-tuple-element.199), kind=kOutput, calls=%fused_computation.1.clone.1 | convolution fusion | flops 408938496 | bytes 14180352 | tf_op jit(solution)/shard_map/while/body/eval_jaxpr/pqhe,pkhe->phqk/dot_general | solution.py:91
  280.1 6.8 %fusion.134 = f32[2,6,512]{2,1,0:T(8,128)S(1)} fusion(f32[2,6,512,512]{3,2,1,0:T(8,128)} %get-tuple-element.172, f32[2,6,512]{2,1,0:T(8,128)S(1)} %select_maximum_fusion.2), kind=kLoop, calls=%fused_computation.3.clone.1 | loop fusion | flops 9431040 | bytes 12632064 | tf_op jit(solution)/shard_map/while/body/eval_jaxpr/reduce_sum | solution.py:99
  301.8 85.9 %all-reduce.4.cloned.1.call-done = bf16[2,512,1536]{2,1,0:T(8,128)(2,1)} async-done(((bf16[2,512,1536]{2,1,0:T(8,128)(2,1)}), bf16[2,512,1536]{2,1,0:T(8,128)(2,1)}) %all-reduce.4.cloned.1.call-update) | async-done | bytes 3145744 | tf_op jit(solution)/shard_map/psum | solution.py:139
  394.4 15.8 %fusion.38 = bf16[2,512,1536]{2,1,0:T(8,128)(2,1)} fusion(bf16[1536,1536]{1,0:T(8,128)(2,1)} %param.27, bf16[1536,1536]{1,0:T(8,128)(2,1)} %param.26, bf16[2,512,1536]{2,1,0:T(8,128)(2,1)} %copy-done.4, f32[2,1536]{1,0:T(2,128)S(1)} %get-tuple-element.113, f32[2,1536]{1,0:T(2,128)S(1)} %get-tuple-element.114, f32[2,512]{1,0:T(2,128)S(1)} %add_rsqrt_fusion.1, ...), kind=kOutput, calls=%fused_computation.50 | convolution fusion | flops 9688842240 | bytes 15761408 | tf_op jit(solution)/shard_map/dot_general | solution.py:31
  410.2 8.7 %copy.44 = bf16[2,512,1536]{1,0,2:T(2,128)(2,1)} copy(bf16[2,512,1536]{2,1,0:T(8,128)(2,1)} %fusion.38) | data formatting | bytes 6291456
  424.2 43.3 %reduce-scatter.4.cloned.1.call-done = bf16[384,1024]{1,0:T(8,128)(2,1)} async-done(((bf16[1536,1024]{1,0:T(8,128)(2,1)}), bf16[384,1024]{1,0:T(8,128)(2,1)}) %reduce-scatter.4.cloned.1.call-update) | async-done | bytes 786448
  472.4 9.1 %all-reduce = (f32[2,512]{1,0:T(2,128)S(1)}, f32[2,512]{1,0:T(2,128)S(1)}) all-reduce(f32[2,512]{1,0:T(2,128)S(1)} %get-tuple-element.69, f32[2,512]{1,0:T(2,128)S(1)} %get-tuple-element.68), channel_id=1, replica_groups=mesh['cfg'=2,'seq'=4,'blk'=4] {'blk'}, use_global_device_ids=true, to_apply=%region_17.18 | all-reduce | flops 2048 | bytes 16384 | tf_op jit(solution)/shard_map/psum | solution.py:154
  482.7 42.1 %all-reduce.6.cloned.1.call-done = bf16[2,512,64]{1,2,0:T(8,128)(2,1)} async-done(((bf16[2,512,64]{1,2,0:T(8,128)(2,1)}), bf16[2,512,64]{1,2,0:T(8,128)(2,1)}) %all-reduce.6.cloned.1.call-update) | async-done | bytes 131088 | tf_op jit(solution)/shard_map/psum | solution.py:172
  527.9 17.2 %pmax.7 = f32[2]{0:T(128)} all-reduce(f32[2]{0:T(128)S(1)} %get-tuple-element.97), channel_id=1, replica_groups=mesh['cfg'=2,'seq'=4,'blk'=4] {'cfg','seq'}, use_global_device_ids=true, to_apply=%region_20.21 | all-reduce | flops 2 | bytes 16 | tf_op jit(solution)/shard_map/pmax | solution.py:183
  (154 shorter events, 87.8 us)
Async XLA Ops:
  7.2 291.0 %copy-start = (bf16[384,1536]{1,0:T(8,128)(2,1)S(1)}, bf16[384,1536]{1,0:T(8,128)(2,1)}, u32[]{:S(2)}) copy-start(bf16[384,1536]{1,0:T(8,128)(2,1)} %param.25) | copy-start | bytes 3538948
  7.2 49.2 %all-gather.10.cloned.1.call-start = ((), (), s32[]{:S(2)}) async-start(), calls=%async_computation.5 | async-start | bytes 3932160 | tf_op jit(solution)/shard_map/all_gather | solution.py:68
  7.9 127.6 %all-gather.8.cloned.1.call-start = ((), (), s32[]{:S(2)}) async-start(), calls=%async_computation.2 | async-start | bytes 3932160 | tf_op jit(solution)/shard_map/all_gather | solution.py:116
  64.3 14.7 %copy-start.15 = (f32[1,2,2,1536]{3,2,1,0:T(2,128)S(1)}, f32[1,2,2,1536]{3,2,1,0:T(2,128)}, u32[]{:S(2)}) copy-start(f32[1,2,2,1536]{3,2,1,0:T(2,128)} %param.21) | copy-start | bytes 73732
  64.3 135.0 %all-gather.6.cloned.1.call-start = ((), (), s32[]{:S(2)}) async-start(), calls=%async_computation.1 | async-start | bytes 3932160 | tf_op jit(solution)/shard_map/all_gather | solution.py:115
  69.3 48.2 %copy-start.19 = (s32[1,2]{1,0:T(1,128)S(1)}, s32[1,2]{1,0:T(1,128)}, u32[]{:S(2)}) copy-start(s32[1,2]{1,0:T(1,128)} %param.30) | copy-start | bytes 28
  69.4 318.3 %all-reduce.4.cloned.1.call-start = ((), (), s32[]{:S(2)}) async-start(), calls=%async_computation.3 | async-start | bytes 6291456 | tf_op jit(solution)/shard_map/psum | solution.py:139
  214.4 6.9 %copy-start.6 = (f32[2,6,512]{2,1,0:T(8,128)S(1)}, f32[2,6,512]{2,1,0:T(8,128)}, u32[]{:S(2)}) copy-start(f32[2,6,512]{2,1,0:T(8,128)} %get-tuple-element.187) | copy-start | bytes 73732 | tf_op jit(solution)/shard_map/while
  214.4 6.9 %copy-start.8 = (f32[2,6,512]{2,1,0:T(8,128)S(1)}, f32[2,6,512]{2,1,0:T(8,128)}, u32[]{:S(2)}) copy-start(f32[2,6,512]{2,1,0:T(8,128)} %get-tuple-element.188) | copy-start | bytes 73732 | tf_op jit(solution)/shard_map/while
  214.4 8.2 %copy-start.1 = (f32[2,6,512,512]{3,2,1,0:T(8,128)S(1)}, f32[2,6,512,512]{3,2,1,0:T(8,128)}, u32[]{:S(2)}) copy-start(f32[2,6,512,512]{3,2,1,0:T(8,128)} %get-tuple-element.172) | copy-start | bytes 37748740 | tf_op jit(solution)/shard_map/while
  236.3 6.9 %copy-start.8 = (f32[2,6,512]{2,1,0:T(8,128)S(1)}, f32[2,6,512]{2,1,0:T(8,128)}, u32[]{:S(2)}) copy-start(f32[2,6,512]{2,1,0:T(8,128)} %get-tuple-element.188) | copy-start | bytes 73732 | tf_op jit(solution)/shard_map/while
  236.3 8.2 %copy-start.1 = (f32[2,6,512,512]{3,2,1,0:T(8,128)S(1)}, f32[2,6,512,512]{3,2,1,0:T(8,128)}, u32[]{:S(2)}) copy-start(f32[2,6,512,512]{3,2,1,0:T(8,128)} %get-tuple-element.172) | copy-start | bytes 37748740 | tf_op jit(solution)/shard_map/while
  258.2 6.9 %copy-start.8 = (f32[2,6,512]{2,1,0:T(8,128)S(1)}, f32[2,6,512]{2,1,0:T(8,128)}, u32[]{:S(2)}) copy-start(f32[2,6,512]{2,1,0:T(8,128)} %get-tuple-element.188) | copy-start | bytes 73732 | tf_op jit(solution)/shard_map/while
  258.2 8.2 %copy-start.1 = (f32[2,6,512,512]{3,2,1,0:T(8,128)S(1)}, f32[2,6,512,512]{3,2,1,0:T(8,128)}, u32[]{:S(2)}) copy-start(f32[2,6,512,512]{3,2,1,0:T(8,128)} %get-tuple-element.172) | copy-start | bytes 37748740 | tf_op jit(solution)/shard_map/while
  280.1 6.9 %copy-start.8 = (f32[2,6,512]{2,1,0:T(8,128)S(1)}, f32[2,6,512]{2,1,0:T(8,128)}, u32[]{:S(2)}) copy-start(f32[2,6,512]{2,1,0:T(8,128)} %get-tuple-element.188) | copy-start | bytes 73732 | tf_op jit(solution)/shard_map/while
  280.1 8.2 %copy-start.1 = (f32[2,6,512,512]{3,2,1,0:T(8,128)S(1)}, f32[2,6,512,512]{3,2,1,0:T(8,128)}, u32[]{:S(2)}) copy-start(f32[2,6,512,512]{3,2,1,0:T(8,128)} %get-tuple-element.172) | copy-start | bytes 37748740 | tf_op jit(solution)/shard_map/while
  301.7 165.8 %reduce-scatter.4.cloned.1.call-start = ((), (), s32[]{:S(2)}) async-start(), calls=%async_computation.6 | async-start | bytes 3932160
  423.3 58.2 %copy-start.18 = (bf16[384,64]{0,1:T(8,128)(2,1)S(1)}, bf16[384,64]{0,1:T(8,128)(2,1)}, u32[]{:S(2)}) copy-start(bf16[384,64]{0,1:T(8,128)(2,1)} %param.28) | copy-start | bytes 147460
  423.3 101.5 %all-reduce.6.cloned.1.call-start = ((), (), s32[]{:S(2)}) async-start(), calls=%async_computation.4 | async-start | bytes 262144 | tf_op jit(solution)/shard_map/psum | solution.py:172
  424.1 101.7 %copy-start.20 = (s32[2]{0:T(128)S(1)}, s32[2]{0:T(128)}, u32[]{:S(2)}) copy-start(s32[2]{0:T(128)} %param.31) | copy-start | bytes 28
  424.2 101.7 %copy-start.21 = (s32[2]{0:T(128)S(1)}, s32[2]{0:T(128)}, u32[]{:S(2)}) copy-start(s32[2]{0:T(128)} %param.32) | copy-start | bytes 28
  424.2 103.0 %copy-start.11 = (f32[2,512,32]{1,2,0:T(8,128)S(1)}, f32[2,512,32]{1,2,0:T(8,128)}, u32[]{:S(2)}) copy-start(f32[2,512,32]{1,2,0:T(8,128)} %param.29) | copy-start | bytes 393220
  424.2 102.9 %copy-start.17 = (f32[2]{0:T(128)S(1)}, f32[2]{0:T(128)}, u32[]{:S(2)}) copy-start(f32[2]{0:T(128)} %param.33) | copy-start | bytes 28
  525.8 1.3 collective-permute-start
  (17 other events, 72.4 us)
Sparse Core Ops, SparseCore 0:
  9.8 46.5 all-gather.9
  64.4 71.0 all-gather.7
  137.1 62.2 all-gather.5
  301.8 85.8 all-reduce.3
  423.4 43.9 reduce-scatter.3
  482.9 41.9 all-reduce.5
where the time goes:
time: 553 us; the launch traced here: 552 us
  waiting for transfers between devices  289 us (52%)
  matrix products  85.7 us (15%)
  blocking collectives  68.6 us (12%)
  other arithmetic  47.8 us (9%)
  local copies, waits for them, and re-layouts  45.9 us (8%)
  between operations  14.5 us (3%)
    psum x1, waiting for transfers between devices, per_device(): lax.psum(attn_part.astype(jnp.bfloat16), 'blk').astype(jnp.float32)  85.9 us
    all_gather x1, waiting for transfers between devices, per_device(): key_piece = lax.all_gather(keys_img, 'seq', axis=1, tiled=True)  59.2 us
    all_gather x1, waiting for transfers between devices, per_device(): lax.all_gather(img_hidden[0], 'blk', axis=2, tiled=True)  46.8 us
    unnamed x7, waiting for transfers between devices  44 us
    psum x1, waiting for transfers between devices, per_device(): lax.psum(velocity_part.astype(jnp.bfloat16), 'blk').astype(jnp.float32)  42.1 us
    dot_general x8, matrix products, project(): result = jnp.dot(flat_rows, weight, preferred_element_type=jnp.float32)  37 us
    dot_general x5, matrix products, attend_block(): jnp.einsum('pqhe,pkhe->phqk', query_heads, key_heads, preferred_element_t...  35.9 us
    reduce_sum x5, other arithmetic, attend_block(): denominator = denominator * factor + jnp.sum(weights, axis=-1)  30.6 us
  transfers between devices with their start and end apart: 7, of which 7 were waited for; matrix products, arithmetic and copies ran while one was open for 5% of the time, Pallas kernels for 0%

commit v1 on v0

--- a/solution.py
+++ b/solution.py
@@ -112,7 +112,12 @@
         jnp.zeros((prompts, head_count, img_rows), jnp.float32),
     )
     running_state = initial
-    key_piece = lax.all_gather(keys_img, "seq", axis=1, tiled=True)
+    ring = [keys_img]
+    for hop in range(3):
+        ring.append(lax.ppermute(ring[-1], "seq", [(dev, (dev + 1) % 4) for dev in range(4)]))
+    key_piece = jnp.roll(
+        jnp.concatenate(ring[::-1], axis=1), (lax.axis_index("seq") + 1) * ring[0].shape[1], axis=1
+    )
     value_piece = lax.all_gather(values_img, "seq", axis=1, tiled=True)
     key_count = key_piece.shape[1]
     blocks = key_count // BLOCK_ROWS

time: 553 us -> 557 us (level)
  waiting for transfers between devices: 289 us -> 247 us
  blocking collectives: 68.6 us -> 100 us
  starting transfers between devices: 0.31 us -> 15.6 us
  matrix products: 85.7 us -> 77.8 us
    all_gather x1 -> x0, waiting for transfers between devices: 59.2 us -> none  [per_device(): key_piece = lax.all_gather(keys_img, 'seq', axis=1, tiled=True)]
    ppermute x0 -> x3, waiting for transfers between devices: none -> 39.7 us  [per_device(): lax.ppermute(ring[-1], 'seq', [(dev, (dev + 1) % 4) for dev in range(4)])]
    all_gather x1, blocking collectives: 16.4 us -> 48.5 us  [per_device(): lax.all_gather(text_keys, 'seq', axis=1, tiled=True)]
    ppermute x0 -> x3, starting transfers between devices: none -> 15.4 us  [per_device(): lax.ppermute(ring[-1], 'seq', [(dev, (dev + 1) % 4) for dev in range(4)])]
    all_gather x1, waiting for transfers between devices: 46.8 us -> 34.9 us  [per_device(): lax.all_gather(img_hidden[0], 'blk', axis=2, tiled=True)]
    all_gather x1, waiting for transfers between devices: 9.59 us -> 0.01 us  [per_device(): value_piece = lax.all_gather(values_img, 'seq', axis=1, tiled=True)]
    add x5, other arithmetic: 0.13 us -> 7.13 us  [attend_block(): denominator = denominator * factor + jnp.sum(weights, axis=-1)]
    dot_general x5, matrix products: 35.9 us -> 28.9 us  [attend_block(): jnp.einsum('pqhe,pkhe->phqk', query_heads, key_heads, preferred_element_t...]
  transfers between devices with their start and end apart: 7 -> 9, of which waited for: 7 -> 7; matrix products, arithmetic and copies ran while one was open for 5% -> 4% of each run, Pallas kernels for 0% -> 0%
where the time goes in v1:
time: 557 us; the launch traced here: 556 us
  waiting for transfers between devices  247 us (44%)
  blocking collectives  100 us (18%)
  matrix products  77.8 us (14%)
  other arithmetic  52.2 us (9%)
  local copies, waits for them, and re-layouts  47.7 us (9%)
  starting transfers between devices  15.6 us (3%)
  between operations  14.3 us (3%)
    psum x1, waiting for transfers between devices, per_device(): lax.psum(attn_part.astype(jnp.bfloat16), 'blk').astype(jnp.float32)  85.6 us
    all_gather x1, blocking collectives, per_device(): lax.all_gather(text_keys, 'seq', axis=1, tiled=True)  48.5 us
    unnamed x6, waiting for transfers between devices  44 us
    psum x1, waiting for transfers between devices, per_device(): lax.psum(velocity_part.astype(jnp.bfloat16), 'blk').astype(jnp.float32)  42.1 us
    ppermute x3, waiting for transfers between devices, per_device(): lax.ppermute(ring[-1], 'seq', [(dev, (dev + 1) % 4) for dev in range(4)])  39.7 us
    dot_general x8, matrix products, project(): result = jnp.dot(flat_rows, weight, preferred_element_type=jnp.float32)  35 us
    all_gather x1, waiting for transfers between devices, per_device(): lax.all_gather(img_hidden[0], 'blk', axis=2, tiled=True)  34.9 us
    reduce_sum x5, other arithmetic, attend_block(): denominator = denominator * factor + jnp.sum(weights, axis=-1)  30.3 us
  transfers between devices with their start and end apart: 9, of which 7 were waited for; matrix products, arithmetic and copies ran while one was open for 4% of the time, Pallas kernels for 0%

profile of v1, /device:TPU:0, one launch (start us, length us, event | category | flops | bytes accessed | tf_op | source)
XLA Modules:
  0.0 555.5 jit_solution(13488916932548445076)
XLA Ops:
  8.9 11.0 %all-gather.1 = bf16[1,2,40,1536]{3,2,1,0:T(8,128)(2,1)S(1)} all-gather(bf16[1,2,40,384]{3,2,1,0:T(8,128)(2,1)} %param.19), channel_id=3, replica_groups=mesh['cfg'=2,'seq'=4,'blk'=4] {'blk'}, dimensions={3}, use_global_device_ids=true | all-gather | bytes 307200 | tf_op jit(solution)/shard_map/all_gather | solution.py:69
  21.5 34.9 %all-gather.7.cloned.1.call-done = bf16[1,2,512,1536]{3,2,1,0:T(8,128)(2,1)} async-done(((bf16[1,2,512,384]{3,2,1,0:T(8,128)(2,1)}), bf16[1,2,512,1536]{3,2,1,0:T(8,128)(2,1)}) %all-gather.7.cloned.1.call-update) | async-done | bytes 3145744 | tf_op jit(solution)/shard_map/all_gather | solution.py:68
  70.5 33.2 %collective-permute-done = bf16[2,512,384]{2,1,0:T(8,128)(2,1)S(1)} collective-permute-done((bf16[2,512,384]{2,1,0:T(8,128)(2,1)S(1)}, bf16[2,512,384]{2,1,0:T(8,128)(2,1)S(1)}, u32[]{:S(2)}, u32[]{:S(2)}) %collective-permute-start) | collective-permute-done | bytes 786464 | tf_op jit(solution)/shard_map/ppermute | solution.py:117
  103.7 12.3 %collective-permute-start.1 = (bf16[2,512,384]{2,1,0:T(8,128)(2,1)S(1)}, bf16[2,512,384]{2,1,0:T(8,128)(2,1)}, u32[]{:S(2)}, u32[]{:S(2)}) collective-permute-start(bf16[2,512,384]{2,1,0:T(8,128)(2,1)S(1)} %collective-permute-done), channel_id=1, source_target_pairs={{0,4},{4,8},{8,12},{12,0},{1,5},{5,9},{9,13},{13,1},{2,6},{6,10},{... | collective-permute-start | bytes 2359304 | tf_op jit(solution)/shard_map/ppermute | solution.py:117
  116.4 48.5 %all_gather.18 = bf16[2,160,384]{2,1,0:T(8,128)(2,1)S(1)} all-gather(bf16[2,40,384]{2,1,0:T(8,128)(2,1)S(1)} %fusion.79), channel_id=1, replica_groups=mesh['cfg'=2,'seq'=4,'blk'=4] {'seq'}, dimensions={1}, use_global_device_ids=true | all-gather | bytes 307200 | tf_op jit(solution)/shard_map/all_gather | solution.py:133
  167.6 14.2 %all_gather.19 = bf16[2,160,384]{2,1,0:T(8,128)(2,1)S(1)} all-gather(bf16[2,40,384]{2,1,0:T(8,128)(2,1)S(1)} %fusion.82), channel_id=1, replica_groups=mesh['cfg'=2,'seq'=4,'blk'=4] {'seq'}, dimensions={1}, use_global_device_ids=true | all-gather | bytes 307200 | tf_op jit(solution)/shard_map/all_gather | solution.py:134
  191.9 6.5 %collective-permute-done.2 = bf16[2,512,384]{2,1,0:T(8,128)(2,1)S(1)} collective-permute-done((bf16[2,512,384]{2,1,0:T(8,128)(2,1)}, bf16[2,512,384]{2,1,0:T(8,128)(2,1)S(1)}, u32[]{:S(2)}, u32[]{:S(2)}) %collective-permute-start.2) | collective-permute-done | bytes 786464 | tf_op jit(solution)/shard_map/ppermute | solution.py:117
  203.8 4.7 copy.36
  208.5 86.4 %while.15 = (s32[]{:T(128)}, f32[2,6,512,64]{2,3,1,0:T(8,128)}, f32[2,6,512]{2,1,0:T(8,128)}, f32[2,6,512]{2,1,0:T(8,128)}, bf16[4,2,512,384]{3,2,0,1:T(8,128)(2...) while((s32[]{:T(128)}, f32[2,6,512,64]{2,3,1,0:T(8,128)}, ...), condition=%wide.region_5.6_spmd.clone, body=%wide.region_2.5_spmd.clone.sunk | while | flops 831682560 | bytes 111378648 | solution.py:131
  210.0 6.4 %bitcast_reduce_fusion.2 = (f32[2,6,512]{2,1,0:T(8,128)S(1)}, f32[2,6,512,512]{3,2,1,0:T(8,128)}) fusion(bf16[2,512,6,64]{1,3,2,0:T(8,128)(2,1)S(1)} %bitcast.166, bf16[2,512,6,64]{1,3,2,0:T(8,128)(2,1)S(1)} %get-tuple-element.207), kind=kOutput, calls=%fused_computation.1.clone.1 | convolution fusion | flops 408938496 | bytes 14180352 | tf_op jit(solution)/shard_map/while/body/eval_jaxpr/pqhe,pkhe->phqk/dot_general | solution.py:91
  216.4 6.8 %fusion.134 = f32[2,6,512]{2,1,0:T(8,128)S(1)} fusion(f32[2,6,512,512]{3,2,1,0:T(8,128)} %get-tuple-element.180, f32[2,6,512]{2,1,0:T(8,128)S(1)} %select_maximum_fusion.2), kind=kLoop, calls=%fused_computation.3.clone.1 | loop fusion | flops 9431040 | bytes 12632064 | tf_op jit(solution)/shard_map/while/body/eval_jaxpr/reduce_sum | solution.py:99
  230.6 6.4 %bitcast_reduce_fusion.2 = (f32[2,6,512]{2,1,0:T(8,128)S(1)}, f32[2,6,512,512]{3,2,1,0:T(8,128)}) fusion(bf16[2,512,6,64]{1,3,2,0:T(8,128)(2,1)S(1)} %bitcast.166, bf16[2,512,6,64]{1,3,2,0:T(8,128)(2,1)S(1)} %get-tuple-element.207), kind=kOutput, calls=%fused_computation.1.clone.1 | convolution fusion | flops 408938496 | bytes 14180352 | tf_op jit(solution)/shard_map/while/body/eval_jaxpr/pqhe,pkhe->phqk/dot_general | solution.py:91
  237.0 6.8 %fusion.134 = f32[2,6,512]{2,1,0:T(8,128)S(1)} fusion(f32[2,6,512,512]{3,2,1,0:T(8,128)} %get-tuple-element.180, f32[2,6,512]{2,1,0:T(8,128)S(1)} %select_maximum_fusion.2), kind=kLoop, calls=%fused_computation.3.clone.1 | loop fusion | flops 9431040 | bytes 12632064 | tf_op jit(solution)/shard_map/while/body/eval_jaxpr/reduce_sum | solution.py:99
  252.5 6.4 %bitcast_reduce_fusion.2 = (f32[2,6,512]{2,1,0:T(8,128)S(1)}, f32[2,6,512,512]{3,2,1,0:T(8,128)}) fusion(bf16[2,512,6,64]{1,3,2,0:T(8,128)(2,1)S(1)} %bitcast.166, bf16[2,512,6,64]{1,3,2,0:T(8,128)(2,1)S(1)} %get-tuple-element.207), kind=kOutput, calls=%fused_computation.1.clone.1 | convolution fusion | flops 408938496 | bytes 14180352 | tf_op jit(solution)/shard_map/while/body/eval_jaxpr/pqhe,pkhe->phqk/dot_general | solution.py:91
  258.9 6.8 %fusion.134 = f32[2,6,512]{2,1,0:T(8,128)S(1)} fusion(f32[2,6,512,512]{3,2,1,0:T(8,128)} %get-tuple-element.180, f32[2,6,512]{2,1,0:T(8,128)S(1)} %select_maximum_fusion.2), kind=kLoop, calls=%fused_computation.3.clone.1 | loop fusion | flops 9431040 | bytes 12632064 | tf_op jit(solution)/shard_map/while/body/eval_jaxpr/reduce_sum | solution.py:99
  274.5 6.4 %bitcast_reduce_fusion.2 = (f32[2,6,512]{2,1,0:T(8,128)S(1)}, f32[2,6,512,512]{3,2,1,0:T(8,128)}) fusion(bf16[2,512,6,64]{1,3,2,0:T(8,128)(2,1)S(1)} %bitcast.166, bf16[2,512,6,64]{1,3,2,0:T(8,128)(2,1)S(1)} %get-tuple-element.207), kind=kOutput, calls=%fused_computation.1.clone.1 | convolution fusion | flops 408938496 | bytes 14180352 | tf_op jit(solution)/shard_map/while/body/eval_jaxpr/pqhe,pkhe->phqk/dot_general | solution.py:91
  280.9 6.8 %fusion.134 = f32[2,6,512]{2,1,0:T(8,128)S(1)} fusion(f32[2,6,512,512]{3,2,1,0:T(8,128)} %get-tuple-element.180, f32[2,6,512]{2,1,0:T(8,128)S(1)} %select_maximum_fusion.2), kind=kLoop, calls=%fused_computation.3.clone.1 | loop fusion | flops 9431040 | bytes 12632064 | tf_op jit(solution)/shard_map/while/body/eval_jaxpr/reduce_sum | solution.py:99
  305.9 85.6 %all-reduce.4.cloned.1.call-done = bf16[2,512,1536]{2,1,0:T(8,128)(2,1)} async-done(((bf16[2,512,1536]{2,1,0:T(8,128)(2,1)}), bf16[2,512,1536]{2,1,0:T(8,128)(2,1)}) %all-reduce.4.cloned.1.call-update) | async-done | bytes 3145744 | tf_op jit(solution)/shard_map/psum | solution.py:144
  398.2 15.9 %fusion.38 = bf16[2,512,1536]{2,1,0:T(8,128)(2,1)} fusion(bf16[1536,1536]{1,0:T(8,128)(2,1)} %param.27, bf16[1536,1536]{1,0:T(8,128)(2,1)} %param.26, bf16[2,512,1536]{2,1,0:T(8,128)(2,1)} %copy-done.6, f32[2,1536]{1,0:T(2,128)S(1)} %get-tuple-element.125, f32[2,1536]{1,0:T(2,128)S(1)} %get-tuple-element.126, f32[2,512]{1,0:T(2,128)S(1)} %add_rsqrt_fusion.1, ...), kind=kOutput, calls=%fused_computation.50 | convolution fusion | flops 9688842240 | bytes 15761408 | tf_op jit(solution)/shard_map/dot_general | solution.py:31
  414.1 8.6 %copy.43 = bf16[2,512,1536]{1,0,2:T(2,128)(2,1)} copy(bf16[2,512,1536]{2,1,0:T(8,128)(2,1)} %fusion.38) | data formatting | bytes 6291456
  428.0 43.3 %reduce-scatter.4.cloned.1.call-done = bf16[384,1024]{1,0:T(8,128)(2,1)} async-done(((bf16[1536,1024]{1,0:T(8,128)(2,1)}), bf16[384,1024]{1,0:T(8,128)(2,1)}) %reduce-scatter.4.cloned.1.call-update) | async-done | bytes 786448
  476.2 9.1 %all-reduce = (f32[2,512]{1,0:T(2,128)S(1)}, f32[2,512]{1,0:T(2,128)S(1)}) all-reduce(f32[2,512]{1,0:T(2,128)S(1)} %get-tuple-element.83, f32[2,512]{1,0:T(2,128)S(1)} %get-tuple-element.82), channel_id=1, replica_groups=mesh['cfg'=2,'seq'=4,'blk'=4] {'blk'}, use_global_device_ids=true, to_apply=%region_17.18 | all-reduce | flops 2048 | bytes 16384 | tf_op jit(solution)/shard_map/psum | solution.py:159
  486.6 42.1 %all-reduce.6.cloned.1.call-done = bf16[2,512,64]{1,2,0:T(8,128)(2,1)} async-done(((bf16[2,512,64]{1,2,0:T(8,128)(2,1)}), bf16[2,512,64]{1,2,0:T(8,128)(2,1)}) %all-reduce.6.cloned.1.call-update) | async-done | bytes 131088 | tf_op jit(solution)/shard_map/psum | solution.py:177
  531.7 17.2 %pmax.7 = f32[2]{0:T(128)} all-reduce(f32[2]{0:T(128)S(1)} %get-tuple-element.109), channel_id=1, replica_groups=mesh['cfg'=2,'seq'=4,'blk'=4] {'cfg','seq'}, use_global_device_ids=true, to_apply=%region_20.21 | all-reduce | flops 2 | bytes 16 | tf_op jit(solution)/shard_map/pmax | solution.py:188
  (183 shorter events, 101.0 us)
Async XLA Ops:
  7.2 295.1 %copy-start = (bf16[384,1536]{1,0:T(8,128)(2,1)S(1)}, bf16[384,1536]{1,0:T(8,128)(2,1)}, u32[]{:S(2)}) copy-start(bf16[384,1536]{1,0:T(8,128)(2,1)} %param.25) | copy-start | bytes 3538948
  7.2 49.2 %all-gather.7.cloned.1.call-start = ((), (), s32[]{:S(2)}) async-start(), calls=%async_computation.4 | async-start | bytes 3932160 | tf_op jit(solution)/shard_map/all_gather | solution.py:68
  7.9 195.9 %all-gather.5.cloned.1.call-start = ((), (), s32[]{:S(2)}) async-start(), calls=%async_computation.1 | async-start | bytes 3932160 | tf_op jit(solution)/shard_map/all_gather | solution.py:121
  21.5 42.9 %copy-start.16 = (f32[2,1536]{1,0:T(2,128)}, f32[2,1536]{1,0:T(2,128)S(1)}, u32[]{:S(2)}) copy-start(f32[2,1536]{1,0:T(2,128)S(1)} %get-tuple-element.127) | copy-start | bytes 36868
  21.5 42.9 %copy-start.17 = (f32[2,1536]{1,0:T(2,128)}, f32[2,1536]{1,0:T(2,128)S(1)}, u32[]{:S(2)}) copy-start(f32[2,1536]{1,0:T(2,128)S(1)} %get-tuple-element.128) | copy-start | bytes 36868
  64.3 327.2 %all-reduce.4.cloned.1.call-start = ((), (), s32[]{:S(2)}) async-start(), calls=%async_computation.2 | async-start | bytes 6291456 | tf_op jit(solution)/shard_map/psum | solution.py:144
  64.4 51.6 %copy-start.22 = (bf16[2,1536,384]{2,1,0:T(8,128)(2,1)S(1)}, bf16[2,1536,384]{2,1,0:T(8,128)(2,1)}, u32[]{:S(2)}) copy-start(bf16[2,1536,384]{2,1,0:T(8,128)(2,1)} %param.24) | copy-start | bytes 7077892
  68.7 114.1 %copy-start.24 = (s32[1,2]{1,0:T(1,128)S(1)}, s32[1,2]{1,0:T(1,128)}, u32[]{:S(2)}) copy-start(s32[1,2]{1,0:T(1,128)} %param.30) | copy-start | bytes 28
  68.7 35.0 %collective-permute-start = (bf16[2,512,384]{2,1,0:T(8,128)(2,1)S(1)}, bf16[2,512,384]{2,1,0:T(8,128)(2,1)S(1)}, u32[]{:S(2)}, u32[]{:S(2)}) collective-permute-start(bf16[2,512,384]{2,1,0:T(8,128)(2,1)S(1)} %convolution_convert_fusion.3), channel_id=1, source_target_pairs={{0,4},{4,8},{8,12},{12,0},{1,5},{5,9},{9,13},{13,1},{2,6},{6,10},{... | collective-permute-start | bytes 2359304 | tf_op jit(solution)/shard_map/ppermute | solution.py:117
  103.7 79.2 %collective-permute-start.1 = (bf16[2,512,384]{2,1,0:T(8,128)(2,1)S(1)}, bf16[2,512,384]{2,1,0:T(8,128)(2,1)}, u32[]{:S(2)}, u32[]{:S(2)}) collective-permute-start(bf16[2,512,384]{2,1,0:T(8,128)(2,1)S(1)} %collective-permute-done), channel_id=1, source_target_pairs={{0,4},{4,8},{8,12},{12,0},{1,5},{5,9},{9,13},{13,1},{2,6},{6,10},{... | collective-permute-start | bytes 2359304 | tf_op jit(solution)/shard_map/ppermute | solution.py:117
  182.9 15.5 %collective-permute-start.2 = (bf16[2,512,384]{2,1,0:T(8,128)(2,1)}, bf16[2,512,384]{2,1,0:T(8,128)(2,1)S(1)}, u32[]{:S(2)}, u32[]{:S(2)}) collective-permute-start(bf16[2,512,384]{2,1,0:T(8,128)(2,1)} %collective-permute-done.1), channel_id=1, source_target_pairs={{0,4},{4,8},{8,12},{12,0},{1,5},{5,9},{9,13},{13,1},{2,6},{6,10},{... | collective-permute-start | bytes 2359304 | tf_op jit(solution)/shard_map/ppermute | solution.py:117
  208.5 87.3 %copy-start.20 = (pred[2,160]{1,0:T(4,128)(4,1)S(1)}, pred[2,160]{1,0:T(4,128)(4,1)}, u32[]{:S(2)}) copy-start(pred[2,160]{1,0:T(4,128)(4,1)} %copy-done.19) | copy-start | bytes 964
  258.9 10.2 %copy-start.1 = (f32[2,6,512,512]{3,2,1,0:T(8,128)S(1)}, f32[2,6,512,512]{3,2,1,0:T(8,128)}, u32[]{:S(2)}) copy-start(f32[2,6,512,512]{3,2,1,0:T(8,128)} %get-tuple-element.180) | copy-start | bytes 37748740 | tf_op jit(solution)/shard_map/while
  258.9 10.2 %copy-start.2 = (f32[2,6,512,64]{2,3,1,0:T(8,128)S(1)}, f32[2,6,512,64]{2,3,1,0:T(8,128)}, u32[]{:S(2)}) copy-start(f32[2,6,512,64]{2,3,1,0:T(8,128)} %get-tuple-element.194) | copy-start | bytes 4718596 | tf_op jit(solution)/shard_map/while
  280.9 10.2 %copy-start.1 = (f32[2,6,512,512]{3,2,1,0:T(8,128)S(1)}, f32[2,6,512,512]{3,2,1,0:T(8,128)}, u32[]{:S(2)}) copy-start(f32[2,6,512,512]{3,2,1,0:T(8,128)} %get-tuple-element.180) | copy-start | bytes 37748740 | tf_op jit(solution)/shard_map/while
  280.9 10.2 %copy-start.2 = (f32[2,6,512,64]{2,3,1,0:T(8,128)S(1)}, f32[2,6,512,64]{2,3,1,0:T(8,128)}, u32[]{:S(2)}) copy-start(f32[2,6,512,64]{2,3,1,0:T(8,128)} %get-tuple-element.194) | copy-start | bytes 4718596 | tf_op jit(solution)/shard_map/while
  305.8 165.5 %reduce-scatter.4.cloned.1.call-start = ((), (), s32[]{:S(2)}) async-start(), calls=%async_computation.5 | async-start | bytes 3932160
  427.2 58.2 %copy-start.23 = (bf16[384,64]{0,1:T(8,128)(2,1)S(1)}, bf16[384,64]{0,1:T(8,128)(2,1)}, u32[]{:S(2)}) copy-start(bf16[384,64]{0,1:T(8,128)(2,1)} %param.28) | copy-start | bytes 147460
  427.2 101.5 %all-reduce.6.cloned.1.call-start = ((), (), s32[]{:S(2)}) async-start(), calls=%async_computation.3 | async-start | bytes 262144 | tf_op jit(solution)/shard_map/psum | solution.py:177
  428.0 101.7 %copy-start.25 = (s32[2]{0:T(128)S(1)}, s32[2]{0:T(128)}, u32[]{:S(2)}) copy-start(s32[2]{0:T(128)} %param.31) | copy-start | bytes 28
  428.0 101.7 %copy-start.26 = (s32[2]{0:T(128)S(1)}, s32[2]{0:T(128)}, u32[]{:S(2)}) copy-start(s32[2]{0:T(128)} %param.32) | copy-start | bytes 28
  428.0 103.0 %copy-start.12 = (f32[2,512,32]{1,2,0:T(8,128)S(1)}, f32[2,512,32]{1,2,0:T(8,128)}, u32[]{:S(2)}) copy-start(f32[2,512,32]{1,2,0:T(8,128)} %param.29) | copy-start | bytes 393220
  428.0 102.9 %copy-start.21 = (f32[2]{0:T(128)S(1)}, f32[2]{0:T(128)}, u32[]{:S(2)}) copy-start(f32[2]{0:T(128)} %param.33) | copy-start | bytes 28
  529.6 1.3 collective-permute-start.3
  (24 other events, 116.6 us)
Sparse Core Ops, SparseCore 0:
  9.8 46.5 all-gather.6
  64.4 95.1 all-gather.4
  306.0 85.5 all-reduce.3
  427.3 43.9 reduce-scatter.3
  486.7 41.9 all-reduce.5
